TPU v7x, 512 devices: a whole 4x4x16 slice. The times are simulated.
512 devices in a mesh: grp: 16 (over x, z_hi, core), slab: 32 (over y, z_lo).
Axes of the slice: x: 4, y: 4, z: 16 (z_hi: 2, z_lo: 8; z = z_hi * 8 + z_lo), core: 2. Of those that a mesh axis runs over, the one named last changes fastest.
Arguments:
- orbitals: bfloat16 [512, 32768], P(('grp', 'slab')), may hold values from -6 to 6
- offsets: int32 [512, 3], replicated, may hold values from 0 to 8
- slot_pairs: int32 [3072, 2], P(('grp', 'slab')), may hold values from -1 to 511, as said below
Outputs:
- exchange_field: float32 [512, 32768], P(('grp', 'slab'))
- gram: float32 [16, 32, 32], P('grp', None, 'slab')
Inputs may be any that keep to these rules, and one draw needn't show every extreme that they name: `slot_pairs`: rows 6 * d to 6 * d + 5 are the slots of device d (grp index times 32 plus slab index). A slot holds two orbital ids i != j, or -1 in both columns when empty. i lies in the slot's group (id // 32); j in the same group or in the next one (group indices wrap). Each group has exactly 160 filled slots, and some device of each group has all 6 slots filled.
All inputs are finite; a program needn't handle non-finite values.
Results may differ from a plain program's by a relative error of at most 0.0003.
Values may be sent and summed in bfloat16 or wider, within the bound.
A program may use at most 64 MiB of HBM per device.

v0:
```python
import functools
import math
import jax
import jax.numpy as jnp
from jax import lax
from jax.sharding import PartitionSpec as P

SIDE = 32
SHIFT = 8
CHEB = 6
stencil_terms = ((1, 1.5), (2, -0.15), (3, 1.0 / 90.0))
center_term = -49.0 / 18.0


def passed_along(block, axis, distance):
    devices = range(lax.axis_size(axis))
    route = [((i - distance) % len(devices), i) for i in devices]
    return lax.ppermute(block, axis, route)


def sent_together(arrays, axis, dim, along):
    ends, at = ([], 0)
    for a in arrays[:-1]:
        at += a.shape[along]
        ends.append(at)
    both = jnp.concatenate(arrays, axis=along)
    return tuple(jnp.split(lax.all_gather(both, axis, axis=dim, tiled=True), ends, axis=along))


def from_everyone(value, axis):
    size = lax.axis_size(axis)
    return lax.all_to_all(
        jnp.broadcast_to(value[None], (size, *value.shape)), axis, 0, 0, tiled=True
    )


def laid_out(blocks, dim):
    shape = list(blocks.shape[1:])
    shape[dim] *= blocks.shape[0]
    return jnp.moveaxis(blocks, 0, dim).reshape(shape)


def gather_directly(value, axis, dim):
    blocks = from_everyone(value, axis)
    return laid_out(blocks, dim)


def in_blocks(value, dim, size):
    before, after = (value.shape[:dim], value.shape[dim + 1 :])
    return jnp.moveaxis(value.reshape(*before, size, -1, *after), dim, 0)


def edges_of(length, count):
    unit = 8 if length >= 8 * count else 1
    return [length // unit * k // count * unit for k in range(1, count)]


def exchange_in_pieces(value, axis, pieces, split_dim, concat_dim):
    blocks = in_blocks(value, split_dim, lax.axis_size(axis))
    cut = max(range(1, max(2, blocks.ndim - 1)), key=lambda d: blocks.shape[d])
    finished = []
    for piece in jnp.split(blocks, edges_of(blocks.shape[cut], pieces), axis=cut):
        if piece.size:
            finished.append(lax.all_to_all(piece, axis, split_axis=0, concat_axis=0, tiled=True))
    return laid_out(jnp.concatenate(finished, axis=cut), concat_dim)


def summed_on_arrival(value, axis, dim):
    size = lax.axis_size(axis)
    blocks = lax.all_to_all(in_blocks(value, dim, size), axis, 0, 0, tiled=True)
    return jnp.sum(blocks, axis=0)


def slide_cells(values, offset, dim_index):
    extent = values.shape[dim_index]
    pad_shape = list(values.shape)
    pad_shape[dim_index] = abs(offset)
    zero_part = jnp.zeros(pad_shape, values.dtype)
    if offset > 0:
        kept_part = lax.slice_in_dim(values, offset, extent, axis=dim_index)
        return jnp.concatenate((kept_part, zero_part), dim_index)
    kept_part = lax.slice_in_dim(values, 0, extent + offset, axis=dim_index)
    return jnp.concatenate((zero_part, kept_part), dim_index)


def operator(values, box_edge):
    outer_dim = values.ndim - 2
    inner_dim = values.ndim - 1
    zcoord = lax.broadcasted_iota(jnp.int32, (box_edge * box_edge,), 0) % box_edge
    stencil_sum = 3.0 * center_term * values
    for offset, weight in stencil_terms:
        beside = slide_cells(values, offset, outer_dim) + slide_cells(values, -offset, outer_dim)
        beside = (
            beside
            + slide_cells(values, offset * box_edge, inner_dim)
            + slide_cells(values, -offset * box_edge, inner_dim)
        )
        upper_part = jnp.where(
            zcoord + offset < box_edge, slide_cells(values, offset, inner_dim), 0.0
        )
        lower_part = jnp.where(zcoord - offset >= 0, slide_cells(values, -offset, inner_dim), 0.0)
        stencil_sum = stencil_sum + weight * (beside + upper_part + lower_part)
    return -stencil_sum


def coefficients(box_edge, sweeps):
    lowest = 3.0 * (math.pi / (box_edge + 1)) ** 2
    highest = 18.2
    center_value = 0.5 * (highest + lowest)
    half_width = 0.5 * (highest - lowest)
    alpha_list = [1.0 / center_value]
    beta_list = [0.0]
    for step_index in range(1, sweeps):
        previous = alpha_list[-1]
        if step_index == 1:
            beta_now = 0.5 * (half_width * previous) ** 2
        else:
            beta_now = (0.5 * half_width * previous) ** 2
        alpha_list.append(1.0 / (center_value - beta_now / previous))
        beta_list.append(beta_now)
    return (alpha_list, beta_list)


def chebyshev_solve(density, box_edge, sweeps):
    alpha_list, beta_list = coefficients(box_edge, sweeps)
    alpha_table = jnp.asarray(alpha_list, jnp.float32)
    beta_table = jnp.asarray(beta_list, jnp.float32)

    def advance(step_index, state):
        solution, residual, search = state
        search = residual + beta_table[step_index] * search
        solution = solution + alpha_table[step_index] * search
        residual = residual - alpha_table[step_index] * operator(search, box_edge)
        return (solution, residual, search)

    start = (jnp.zeros_like(density), density, jnp.zeros_like(density))
    return lax.fori_loop(0, sweeps, advance, start)[0]


def place_box(box, offset_gap, box_edge, margin):
    cube = box.reshape(box_edge, box_edge, box_edge)
    padded = jnp.pad(cube, margin)
    start = margin - offset_gap
    moved = lax.dynamic_slice(
        padded, (start[0], start[1], start[2]), (box_edge, box_edge, box_edge)
    )
    return moved.reshape(box_edge, box_edge * box_edge)


def on_device(orbitals, offsets, slot_pairs):
    box_edge = SIDE
    cell_count = orbitals.shape[1]
    shaped = functools.partial(place_box, box_edge=box_edge, margin=SHIFT)
    members = lax.axis_size("slab")
    group_count = lax.axis_size("grp")
    group_index = lax.axis_index("grp")
    member_index = lax.axis_index("slab")
    next_box = passed_along(orbitals, "grp", -1)
    near_boxes, far_boxes = sent_together((orbitals, next_box), "slab", 0, 1)
    listing = gather_directly(slot_pairs, "slab", 0)
    live_flags = listing[:, 0] >= 0
    live_ranks = jnp.cumsum(live_flags.astype(jnp.int32)) - 1
    slot_quota = -(-(5 * members) // members)
    targets = member_index * slot_quota + jnp.arange(slot_quota, dtype=jnp.int32)
    select = live_flags[None, :] & (live_ranks[None, :] == targets[:, None])
    chosen_pairs = jnp.sum(jnp.where(select[:, :, None], listing[None, :, :], 0), axis=1)
    live_slot = jnp.any(select, axis=1)
    first_id = group_index * members
    second_id = (group_index + 1) % group_count * members
    own_id = first_id + member_index
    left_id = jnp.where(live_slot, chosen_pairs[:, 0], own_id)
    right_id = jnp.where(live_slot, chosen_pairs[:, 1], own_id)
    left_row = left_id - first_id
    right_row = jnp.where(
        right_id // members == group_index, right_id - first_id, members + right_id - second_id
    )
    box_table = jnp.concatenate((near_boxes, far_boxes), 0)
    offset_gap = offsets[right_id] - offsets[left_id]
    left_box = box_table[left_row].reshape(-1, box_edge, box_edge * box_edge).astype(jnp.float32)
    right_box = jax.vmap(shaped)(box_table[right_row], offset_gap).astype(jnp.float32)
    density = left_box * right_box * live_slot.astype(jnp.float32)[:, None, None]
    potential = chebyshev_solve(density, box_edge, CHEB)
    to_left = (potential * right_box).reshape(-1, cell_count)
    to_right = jax.vmap(shaped)(potential * left_box, -offset_gap).reshape(-1, cell_count)
    partial_fields = jnp.zeros((2 * members, cell_count), jnp.float32)
    partial_fields = partial_fields.at[left_row].add(to_left).at[right_row].add(to_right)
    incoming = passed_along(partial_fields[members:], "grp", 1)
    merged = exchange_in_pieces(partial_fields[:members] + incoming, "slab", 2, 0, 0)
    exchange_field = jnp.sum(merged, 0, keepdims=True)
    anchor = offsets[first_id]
    own_shift = offsets[own_id] - anchor
    framed_field = shaped(exchange_field[0], own_shift).astype(jnp.bfloat16).reshape(1, cell_count)
    norm_factor = 1.0 / math.sqrt(cell_count)
    framed_orbital = shaped(orbitals[0], own_shift).reshape(1, cell_count)
    orbital_slabs, field_slabs = (
        lax.all_to_all(framed_orbital, "slab", split_axis=1, concat_axis=0, tiled=True),
        lax.all_to_all(framed_field, "slab", split_axis=1, concat_axis=0, tiled=True),
    )
    partial_gram = (
        lax.dot_general(
            orbital_slabs, field_slabs, (((1,), (1,)), ((), ())), preferred_element_type=jnp.float32
        )
        * norm_factor
    )
    column = summed_on_arrival(partial_gram, "slab", 1)
    gram_block = column.reshape(1, members, 1)
    return (exchange_field, gram_block)


def solution(mesh):
    return jax.shard_map(
        on_device,
        mesh=mesh,
        in_specs=(P(("grp", "slab"), None), P(), P(("grp", "slab"), None)),
        out_specs=(P(("grp", "slab"), None), P("grp", None, "slab")),
        check_vma=False,
    )
```

profile of v0, /device:TPU:2, one launch (start us, length us, event | category | flops | bytes accessed | tf_op | source)
XLA Modules:
  0.0 873.7 jit_solution(8631526173494886654)
XLA Ops:
  7.2 15.1 %collective-permute-start = (bf16[1,32768]{1,0:T(2,128)(2,1)}, bf16[1,32768]{1,0:T(2,128)(2,1)S(1)}, u32[]{:S(2)}, u32[]{:S(2)}) collective-permute-start(bf16[1,32768]{1,0:T(2,128)(2,1)} %param.7), channel_id=1, source_target_pairs={{32,0},{64,32},{96,64},{128,96},{160,128},{192,160},{224,192},{256... | collective-permute-start | bytes 196616 | tf_op jit(solution)/shard_map/ppermute | solution.py:18
  28.7 9.3 %all-to-all-start = ((s32[32,6,2]{1,2,0:T(2,128)}), s32[32,6,2]{1,2,0:T(2,128)S(1)}, u32[]{:S(2)}, u32[]{:S(2)}) async-start(s32[32,6,2]{1,2,0:T(2,128)} %broadcast_in_dim.132), calls=%async_computation | async-start | bytes 65536 | tf_op jit(solution)/shard_map/all_to_all | solution.py:32
  38.9 11.6 %all-to-all-done = s32[32,6,2]{1,2,0:T(2,128)S(1)} async-done(((s32[32,6,2]{1,2,0:T(2,128)}), s32[32,6,2]{1,2,0:T(2,128)S(1)}, u32[]{:S(2)}, u32[]{:S(2)}) %all-to-all-start) | async-done | bytes 1568 | tf_op jit(solution)/shard_map/all_to_all | solution.py:32
  53.4 237.7 %all-gather.3.cloned.1.call-done = bf16[32,1,65536]{2,1,0:T(2,128)(2,1)} async-done(((bf16[1,1,65536]{2,1,0:T(2,128)(2,1)}), bf16[32,1,65536]{2,1,0:T(2,128)(2,1)}) %all-gather.3.cloned.1.call-update) | async-done | bytes 4194320 | tf_op jit(solution)/shard_map/all_gather | solution.py:27
  291.1 8.0 copy.77
  301.6 3.8 gather_fusion.1
  308.6 25.1 %while.23 = (s32[]{:T(128)}, bf16[5,48,48,48]{3,2,1,0:T(8,128)(2,1)}, s32[5,4]{1,0:T(8,128)S(1)}, bf16[5,32,32,32]{3,2,1,0:T(8,128)(2,1)}, s32[]{:T(128)}) while((s32[]{:T(128)}, bf16[5,48,48,48]{3,2,1,0:T(8,128)(2,1)}, s32[5,4]{1,0:T(8,128)S(1)}, bf16[5,32,32,32]{3,2,1,0:T(8,128)(2,1)}, s32[]{:T(128)}) %tuple.145), condition=%wide.while_cond, body=%wide.while_body.sunk | while | flops 2 | bytes 526977 | solution.py:144
  309.2 4.4 dynamic-slice_dynamic-update-slice_fusion.4
  314.3 4.4 dynamic-slice_dynamic-update-slice_fusion.4
  319.3 4.4 dynamic-slice_dynamic-update-slice_fusion.4
  324.3 4.3 dynamic-slice_dynamic-update-slice_fusion.4
  329.3 4.4 dynamic-slice_dynamic-update-slice_fusion.4
  336.9 3.8 gather_fusion
  342.4 42.8 %while.25 = (s32[]{:T(128)}, f32[5,32,1024]{2,1,0:T(8,128)S(1)}, f32[5,32,1024]{2,1,0:T(8,128)S(1)}, f32[5,32,1024]{2,1,0:T(8,128)S(1)}, s32[]{:T(128)}, /*index=5*/f32[6]{0:T(128)S(1)}, s32[]{:T(128)}, f32[6]{0:T(128)S(1)}) while((s32[]{:T(128)}, f32[5,32,1024]{2,1,0:T(8,128)S(1)}, f32[5,32,1024]{2,1,0:T(8,128)S(1)}, ...), condition=%wide.region_5.6_spmd.clone.clone, body=%wide.region_4.5_spmd.sunk.clone.clone.sunk | while | flops 6092803 | bytes 39147136 | solution.py:137
  393.3 26.0 %while.24 = (s32[]{:T(128)}, f32[5,48,48,48]{3,2,1,0:T(8,128)}, s32[5,4]{1,0:T(8,128)S(1)}, f32[5,32,32,32]{3,2,1,0:T(8,128)}, s32[]{:T(128)}) while((s32[]{:T(128)}, f32[5,48,48,48]{3,2,1,0:T(8,128)}, s32[5,4]{1,0:T(8,128)S(1)}, f32[5,32,32,32]{3,2,1,0:T(8,128)}, s32[]{:T(128)}) %tuple.151), condition=%wide.while_cond.1, body=%wide.while_body.1.sunk | while | flops 2 | bytes 1051265 | solution.py:144
  393.9 4.6 dynamic-slice_dynamic-update-slice_fusion.5
  399.1 4.6 dynamic-slice_dynamic-update-slice_fusion.5
  404.4 4.6 dynamic-slice_dynamic-update-slice_fusion.5
  409.5 4.6 dynamic-slice_dynamic-update-slice_fusion.5
  414.7 4.6 dynamic-slice_dynamic-update-slice_fusion.5
  422.5 5.0 scatter_custom_fusion
  427.5 8.1 scatter_fusion
  440.4 114.9 %collective-permute-done.1 = f32[32,32768]{1,0:T(8,128)S(1)} collective-permute-done((f32[32,32768]{1,0:T(8,128)S(1)}, f32[32,32768]{1,0:T(8,128)S(1)}, u32[]{:S(2)}, u32[]{:S(2)}) %collective-permute-start.1) | collective-permute-done | bytes 4194336 | tf_op jit(solution)/shard_map/ppermute | solution.py:18
  555.8 4.0 reshape.153
  559.8 71.3 %all-to-all-start.1 = ((f32[32,1,32768]{2,1,0:T(1,128)}), f32[32,1,32768]{2,1,0:T(1,128)}, u32[]{:S(2)}, u32[]{:S(2)}) async-start(f32[32,1,32768]{2,1,0:T(1,128)} %reshape.153), calls=%async_computation.1 | async-start | bytes 8388608 | tf_op jit(solution)/shard_map/all_to_all | solution.py:64
  640.7 162.0 %all-to-all-done.1 = f32[32,1,32768]{2,1,0:T(1,128)} async-done(((f32[32,1,32768]{2,1,0:T(1,128)}), f32[32,1,32768]{2,1,0:T(1,128)}, u32[]{:S(2)}, u32[]{:S(2)}) %all-to-all-start.1) | async-done | bytes 4194336 | tf_op jit(solution)/shard_map/all_to_all | solution.py:64
  802.8 14.4 %all-to-all-start.2 = ((bf16[32,2,512]{2,1,0:T(2,128)(2,1)}), bf16[32,2,512]{2,1,0:T(2,128)(2,1)S(1)}, u32[]{:S(2)}, u32[]{:S(2)}) async-start(bf16[32,2,512]{2,1,0:T(2,128)(2,1)} %reshape.274), calls=%async_computation.2 | async-start | bytes 131072 | tf_op jit(solution)/shard_map/all_to_all | solution.py:196
  817.2 4.9 reduce_sum.28
  824.6 5.2 all-to-all-done.2
  829.8 7.3 all-to-all-start.3
  837.2 12.6 %all-to-all-done.3 = bf16[32,2,512]{2,1,0:T(2,128)(2,1)S(1)} async-done(((bf16[32,2,512]{2,1,0:T(2,128)(2,1)}), bf16[32,2,512]{2,1,0:T(2,128)(2,1)S(1)}, u32[]{:S(2)}, u32[]{:S(2)}) %all-to-all-start.3) | async-done | bytes 65568 | tf_op jit(solution)/shard_map/all_to_all | solution.py:197
  850.0 16.2 %all_to_all.45 = f32[32,32,1]{1,2,0:T(1,128)S(1)} all-to-all(f32[32,32,1]{1,2,0:T(1,128)S(1)} %copy.50), channel_id=1, replica_groups=mesh['grp'=16,'slab'=32] {'slab'}, dimensions={0} | all-to-all | bytes 8192 | tf_op jit(solution)/shard_map/all_to_all | solution.py:70
  (199 shorter events, 93.2 us)
Async XLA Ops:
  7.2 284.0 %all-gather.3.cloned.1.call-start = ((), (), s32[]{:S(2)}) async-start(), calls=%async_computation.5 | async-start | bytes 8650752 | tf_op jit(solution)/shard_map/all_gather | solution.py:27
  7.2 18.3 %collective-permute-start = (bf16[1,32768]{1,0:T(2,128)(2,1)}, bf16[1,32768]{1,0:T(2,128)(2,1)S(1)}, u32[]{:S(2)}, u32[]{:S(2)}) collective-permute-start(bf16[1,32768]{1,0:T(2,128)(2,1)} %param.7), channel_id=1, source_target_pairs={{32,0},{64,32},{96,64},{128,96},{160,128},{192,160},{224,192},{256... | collective-permute-start | bytes 196616 | tf_op jit(solution)/shard_map/ppermute | solution.py:18
  28.7 21.8 %all-to-all-start = ((s32[32,6,2]{1,2,0:T(2,128)}), s32[32,6,2]{1,2,0:T(2,128)S(1)}, u32[]{:S(2)}, u32[]{:S(2)}) async-start(s32[32,6,2]{1,2,0:T(2,128)} %broadcast_in_dim.132), calls=%async_computation | async-start | bytes 65536 | tf_op jit(solution)/shard_map/all_to_all | solution.py:32
  336.9 5.4 copy-start.5
  336.9 5.4 copy-start.6
  393.3 28.8 %copy-start.1 = (f32[1,5,32,1024]{3,2,1,0:T(8,128)S(1)}, f32[1,5,32,1024]{3,2,1,0:T(8,128)}, u32[]{:S(2)}) copy-start(f32[1,5,32,1024]{3,2,1,0:T(8,128)} %get-tuple-element.316) | copy-start | bytes 1966084
  435.6 119.8 %copy-start = (f32[64,32768]{1,0:T(8,128)S(1)}, f32[64,32768]{1,0:T(8,128)}, u32[]{:S(2)}) copy-start(f32[64,32768]{1,0:T(8,128)} %scatter_fusion) | copy-start | bytes 25165828
  438.2 117.1 %collective-permute-start.1 = (f32[32,32768]{1,0:T(8,128)S(1)}, f32[32,32768]{1,0:T(8,128)S(1)}, u32[]{:S(2)}, u32[]{:S(2)}) collective-permute-start(f32[32,32768]{1,0:T(8,128)S(1)} %slice.373), channel_id=1, source_target_pairs={{480,0},{0,32},{32,64},{64,96},{96,128},{128,160},{160,192},{192,2... | collective-permute-start | bytes 12582920 | tf_op jit(solution)/shard_map/ppermute | solution.py:18
  559.8 71.4 %copy-start.4 = (s32[512,3]{0,1:T(4,128)S(1)}, s32[512,3]{0,1:T(4,128)}, u32[]{:S(2)}) copy-start(s32[512,3]{0,1:T(4,128)} %param.8) | copy-start | bytes 18436
  559.8 75.7 %copy-start.3 = (bf16[1,32768]{1,0:T(2,128)(2,1)S(1)}, bf16[1,32768]{1,0:T(2,128)(2,1)}, u32[]{:S(2)}) copy-start(bf16[1,32768]{1,0:T(2,128)(2,1)} %param.7) | copy-start | bytes 196612
  559.8 243.0 %all-to-all-start.1 = ((f32[32,1,32768]{2,1,0:T(1,128)}), f32[32,1,32768]{2,1,0:T(1,128)}, u32[]{:S(2)}, u32[]{:S(2)}) async-start(f32[32,1,32768]{2,1,0:T(1,128)} %reshape.153), calls=%async_computation.1 | async-start | bytes 8388608 | tf_op jit(solution)/shard_map/all_to_all | solution.py:64
  802.8 27.0 %all-to-all-start.2 = ((bf16[32,2,512]{2,1,0:T(2,128)(2,1)}), bf16[32,2,512]{2,1,0:T(2,128)(2,1)S(1)}, u32[]{:S(2)}, u32[]{:S(2)}) async-start(bf16[32,2,512]{2,1,0:T(2,128)(2,1)} %reshape.274), calls=%async_computation.2 | async-start | bytes 131072 | tf_op jit(solution)/shard_map/all_to_all | solution.py:196
  822.1 44.7 %copy-start.2 = (f32[32768]{0:T(1024)}, f32[32768]{0:T(1024)S(1)}, u32[]{:S(2)}) copy-start(f32[32768]{0:T(1024)S(1)} %reduce_sum.28) | copy-start | bytes 393220
  829.8 20.0 %all-to-all-start.3 = ((bf16[32,2,512]{2,1,0:T(2,128)(2,1)}), bf16[32,2,512]{2,1,0:T(2,128)(2,1)S(1)}, u32[]{:S(2)}, u32[]{:S(2)}) async-start(bf16[32,2,512]{2,1,0:T(2,128)(2,1)} %reshape.272), calls=%async_computation.3 | async-start | bytes 131072 | tf_op jit(solution)/shard_map/all_to_all | solution.py:197
Sparse Core Ops, SparseCore 0:
  27.5 263.5 all-gather.2
where the time goes:
time: 875 us; the launch traced here: 874 us
  waiting for transfers between devices  547 us (63%)
  starting transfers between devices  120 us (14%)
  local copies, waits for them, and re-layouts  114 us (13%)
  other arithmetic  55.6 us (6%)
  between operations  20 us (2%)
  blocking collectives  16.2 us (2%)
    all_gather x1, waiting for transfers between devices, sent_together(): lax.all_gather(both, axis, axis=dim, tiled=True)  238 us
    all_to_all x1, waiting for transfers between devices, exchange_in_pieces(): lax.all_to_all(piece, axis, split_axis=0, concat_axis=0, tiled=True)  162 us
    ppermute x2, waiting for transfers between devices, passed_along(): return lax.ppermute(block, axis, route)  118 us
    all_to_all x1, starting transfers between devices, exchange_in_pieces(): lax.all_to_all(piece, axis, split_axis=0, concat_axis=0, tiled=True)  71.3 us
    gather x30, local copies, waits for them, and re-layouts  51 us
  transfers between devices with their start and end apart: 7, of which 7 were waited for; matrix products, arithmetic and copies ran while one was open for 2% of the time, Pallas kernels for 0%

commit v1 on v0

--- a/solution.py
+++ b/solution.py
@@ -148,6 +148,18 @@
 
 
 def on_device(orbitals, offsets, slot_pairs):
+
+    def close_patch_here(here_x, ax_name):
+        return jnp.concatenate(
+            lax.all_to_all(
+                jnp.stack(jnp.split(here_x, lax.axis_size(ax_name), 1), axis=0),
+                ax_name,
+                split_axis=0,
+                concat_axis=0,
+            ),
+            0,
+        )
+
     box_edge = SIDE
     cell_count = orbitals.shape[1]
     shaped = functools.partial(place_box, box_edge=box_edge, margin=SHIFT)
@@ -194,7 +206,7 @@
     framed_orbital = shaped(orbitals[0], own_shift).reshape(1, cell_count)
     orbital_slabs, field_slabs = (
         lax.all_to_all(framed_orbital, "slab", split_axis=1, concat_axis=0, tiled=True),
-        lax.all_to_all(framed_field, "slab", split_axis=1, concat_axis=0, tiled=True),
+        close_patch_here(framed_field, "slab"),
     )
     partial_gram = (
         lax.dot_general(

time: 875 us -> 876 us (level)
  no operation moved by 1% of the time
where the time goes in v1:
time: 876 us; the launch traced here: 874 us
  waiting for transfers between devices  547 us (62%)
  starting transfers between devices  120 us (14%)
  local copies, waits for them, and re-layouts  115 us (13%)
  other arithmetic  55.6 us (6%)
  between operations  20.1 us (2%)
  blocking collectives  16.2 us (2%)
    all_gather x1, waiting for transfers between devices, sent_together(): lax.all_gather(both, axis, axis=dim, tiled=True)  238 us
    all_to_all x1, waiting for transfers between devices, exchange_in_pieces(): lax.all_to_all(piece, axis, split_axis=0, concat_axis=0, tiled=True)  162 us
    ppermute x2, waiting for transfers between devices, passed_along(): return lax.ppermute(block, axis, route)  118 us
    all_to_all x1, starting transfers between devices, exchange_in_pieces(): lax.all_to_all(piece, axis, split_axis=0, concat_axis=0, tiled=True)  71.3 us
    gather x30, local copies, waits for them, and re-layouts  51 us
  transfers between devices with their start and end apart: 7, of which 7 were waited for; matrix products, arithmetic and copies ran while one was open for 2% of the time, Pallas kernels for 0%

profile of v1, /device:TPU:2, one launch (start us, length us, event | category | flops | bytes accessed | tf_op | source)
XLA Modules:
  0.0 874.2 jit_solution(18266301814595298100)
XLA Ops:
  7.2 15.1 %collective-permute-start = (bf16[1,32768]{1,0:T(2,128)(2,1)}, bf16[1,32768]{1,0:T(2,128)(2,1)S(1)}, u32[]{:S(2)}, u32[]{:S(2)}) collective-permute-start(bf16[1,32768]{1,0:T(2,128)(2,1)} %param.7), channel_id=1, source_target_pairs={{32,0},{64,32},{96,64},{128,96},{160,128},{192,160},{224,192},{256... | collective-permute-start | bytes 196616 | tf_op jit(solution)/shard_map/ppermute | solution.py:18
  28.7 9.3 %all-to-all-start = ((s32[32,6,2]{1,2,0:T(2,128)}), s32[32,6,2]{1,2,0:T(2,128)S(1)}, u32[]{:S(2)}, u32[]{:S(2)}) async-start(s32[32,6,2]{1,2,0:T(2,128)} %broadcast_in_dim.132), calls=%async_computation | async-start | bytes 65536 | tf_op jit(solution)/shard_map/all_to_all | solution.py:32
  38.9 11.6 %all-to-all-done = s32[32,6,2]{1,2,0:T(2,128)S(1)} async-done(((s32[32,6,2]{1,2,0:T(2,128)}), s32[32,6,2]{1,2,0:T(2,128)S(1)}, u32[]{:S(2)}, u32[]{:S(2)}) %all-to-all-start) | async-done | bytes 1568 | tf_op jit(solution)/shard_map/all_to_all | solution.py:32
  53.4 237.7 %all-gather.3.cloned.1.call-done = bf16[32,1,65536]{2,1,0:T(2,128)(2,1)} async-done(((bf16[1,1,65536]{2,1,0:T(2,128)(2,1)}), bf16[32,1,65536]{2,1,0:T(2,128)(2,1)}) %all-gather.3.cloned.1.call-update) | async-done | bytes 4194320 | tf_op jit(solution)/shard_map/all_gather | solution.py:27
  291.1 8.0 copy.75
  301.6 3.8 gather_fusion.1
  308.6 25.1 %while.23 = (s32[]{:T(128)}, bf16[5,48,48,48]{3,2,1,0:T(8,128)(2,1)}, s32[5,4]{1,0:T(8,128)S(1)}, bf16[5,32,32,32]{3,2,1,0:T(8,128)(2,1)}, s32[]{:T(128)}) while((s32[]{:T(128)}, bf16[5,48,48,48]{3,2,1,0:T(8,128)(2,1)}, s32[5,4]{1,0:T(8,128)S(1)}, bf16[5,32,32,32]{3,2,1,0:T(8,128)(2,1)}, s32[]{:T(128)}) %tuple.145), condition=%wide.while_cond, body=%wide.while_body.sunk | while | flops 2 | bytes 526977 | solution.py:144
  309.2 4.4 dynamic-slice_dynamic-update-slice_fusion.4
  314.3 4.4 dynamic-slice_dynamic-update-slice_fusion.4
  319.3 4.4 dynamic-slice_dynamic-update-slice_fusion.4
  324.3 4.3 dynamic-slice_dynamic-update-slice_fusion.4
  329.3 4.4 dynamic-slice_dynamic-update-slice_fusion.4
  336.9 3.8 gather_fusion
  342.4 42.8 %while.25 = (s32[]{:T(128)}, f32[5,32,1024]{2,1,0:T(8,128)S(1)}, f32[5,32,1024]{2,1,0:T(8,128)S(1)}, f32[5,32,1024]{2,1,0:T(8,128)S(1)}, s32[]{:T(128)}, /*index=5*/f32[6]{0:T(128)S(1)}, s32[]{:T(128)}, f32[6]{0:T(128)S(1)}) while((s32[]{:T(128)}, f32[5,32,1024]{2,1,0:T(8,128)S(1)}, f32[5,32,1024]{2,1,0:T(8,128)S(1)}, ...), condition=%wide.region_5.6_spmd.clone.clone, body=%wide.region_4.5_spmd.sunk.clone.clone.sunk | while | flops 6092803 | bytes 39147136 | solution.py:137
  393.3 26.0 %while.24 = (s32[]{:T(128)}, f32[5,48,48,48]{3,2,1,0:T(8,128)}, s32[5,4]{1,0:T(8,128)S(1)}, f32[5,32,32,32]{3,2,1,0:T(8,128)}, s32[]{:T(128)}) while((s32[]{:T(128)}, f32[5,48,48,48]{3,2,1,0:T(8,128)}, s32[5,4]{1,0:T(8,128)S(1)}, f32[5,32,32,32]{3,2,1,0:T(8,128)}, s32[]{:T(128)}) %tuple.151), condition=%wide.while_cond.1, body=%wide.while_body.1.sunk | while | flops 2 | bytes 1051265 | solution.py:144
  393.9 4.6 dynamic-slice_dynamic-update-slice_fusion.5
  399.1 4.6 dynamic-slice_dynamic-update-slice_fusion.5
  404.4 4.6 dynamic-slice_dynamic-update-slice_fusion.5
  409.5 4.6 dynamic-slice_dynamic-update-slice_fusion.5
  414.7 4.6 dynamic-slice_dynamic-update-slice_fusion.5
  422.5 5.0 scatter_custom_fusion
  427.5 8.1 scatter_fusion
  440.4 114.9 %collective-permute-done.1 = f32[32,32768]{1,0:T(8,128)S(1)} collective-permute-done((f32[32,32768]{1,0:T(8,128)S(1)}, f32[32,32768]{1,0:T(8,128)S(1)}, u32[]{:S(2)}, u32[]{:S(2)}) %collective-permute-start.1) | collective-permute-done | bytes 4194336 | tf_op jit(solution)/shard_map/ppermute | solution.py:18
  555.8 4.0 reshape.149
  559.8 71.3 %all-to-all-start.1 = ((f32[32,1,32768]{2,1,0:T(1,128)}), f32[32,1,32768]{2,1,0:T(1,128)}, u32[]{:S(2)}, u32[]{:S(2)}) async-start(f32[32,1,32768]{2,1,0:T(1,128)} %reshape.149), calls=%async_computation.1 | async-start | bytes 8388608 | tf_op jit(solution)/shard_map/all_to_all | solution.py:64
  640.7 162.0 %all-to-all-done.1 = f32[32,1,32768]{2,1,0:T(1,128)} async-done(((f32[32,1,32768]{2,1,0:T(1,128)}), f32[32,1,32768]{2,1,0:T(1,128)}, u32[]{:S(2)}, u32[]{:S(2)}) %all-to-all-start.1) | async-done | bytes 4194336 | tf_op jit(solution)/shard_map/all_to_all | solution.py:64
  802.8 14.4 %all-to-all-start.2 = ((bf16[32,2,512]{2,1,0:T(2,128)(2,1)}), bf16[32,2,512]{2,1,0:T(2,128)(2,1)S(1)}, u32[]{:S(2)}, u32[]{:S(2)}) async-start(bf16[32,2,512]{2,1,0:T(2,128)(2,1)} %reshape.271), calls=%async_computation.2 | async-start | bytes 131072 | tf_op jit(solution)/shard_map/all_to_all | solution.py:208
  817.2 4.9 reduce_sum.28
  825.1 4.7 all-to-all-done.2
  829.8 7.8 all-to-all-start.3
  837.7 12.6 %all-to-all-done.3 = bf16[32,2,512]{2,1,0:T(2,128)(2,1)S(1)} async-done(((bf16[32,2,512]{2,1,0:T(2,128)(2,1)}), bf16[32,2,512]{2,1,0:T(2,128)(2,1)S(1)}, u32[]{:S(2)}, u32[]{:S(2)}) %all-to-all-start.3) | async-done | bytes 65568 | tf_op jit(solution)/shard_map/all_to_all | solution.py:154
  850.5 16.2 %all_to_all.37 = f32[32,32,1]{1,2,0:T(1,128)S(1)} all-to-all(f32[32,32,1]{1,2,0:T(1,128)S(1)} %copy.48), channel_id=1, replica_groups=mesh['grp'=16,'slab'=32] {'slab'}, dimensions={0} | all-to-all | bytes 8192 | tf_op jit(solution)/shard_map/all_to_all | solution.py:70
  (231 shorter events, 93.6 us)
Async XLA Ops:
  7.2 284.0 %all-gather.3.cloned.1.call-start = ((), (), s32[]{:S(2)}) async-start(), calls=%async_computation.5 | async-start | bytes 8650752 | tf_op jit(solution)/shard_map/all_gather | solution.py:27
  7.2 18.3 %collective-permute-start = (bf16[1,32768]{1,0:T(2,128)(2,1)}, bf16[1,32768]{1,0:T(2,128)(2,1)S(1)}, u32[]{:S(2)}, u32[]{:S(2)}) collective-permute-start(bf16[1,32768]{1,0:T(2,128)(2,1)} %param.7), channel_id=1, source_target_pairs={{32,0},{64,32},{96,64},{128,96},{160,128},{192,160},{224,192},{256... | collective-permute-start | bytes 196616 | tf_op jit(solution)/shard_map/ppermute | solution.py:18
  28.7 21.8 %all-to-all-start = ((s32[32,6,2]{1,2,0:T(2,128)}), s32[32,6,2]{1,2,0:T(2,128)S(1)}, u32[]{:S(2)}, u32[]{:S(2)}) async-start(s32[32,6,2]{1,2,0:T(2,128)} %broadcast_in_dim.132), calls=%async_computation | async-start | bytes 65536 | tf_op jit(solution)/shard_map/all_to_all | solution.py:32
  336.9 5.4 copy-start.5
  336.9 5.4 copy-start.6
  393.3 28.8 %copy-start.1 = (f32[1,5,32,1024]{3,2,1,0:T(8,128)S(1)}, f32[1,5,32,1024]{3,2,1,0:T(8,128)}, u32[]{:S(2)}) copy-start(f32[1,5,32,1024]{3,2,1,0:T(8,128)} %get-tuple-element.316) | copy-start | bytes 1966084
  435.6 119.8 %copy-start = (f32[64,32768]{1,0:T(8,128)S(1)}, f32[64,32768]{1,0:T(8,128)}, u32[]{:S(2)}) copy-start(f32[64,32768]{1,0:T(8,128)} %scatter_fusion) | copy-start | bytes 25165828
  438.2 117.1 %collective-permute-start.1 = (f32[32,32768]{1,0:T(8,128)S(1)}, f32[32,32768]{1,0:T(8,128)S(1)}, u32[]{:S(2)}, u32[]{:S(2)}) collective-permute-start(f32[32,32768]{1,0:T(8,128)S(1)} %slice.373), channel_id=1, source_target_pairs={{480,0},{0,32},{32,64},{64,96},{96,128},{128,160},{160,192},{192,2... | collective-permute-start | bytes 12582920 | tf_op jit(solution)/shard_map/ppermute | solution.py:18
  559.8 71.4 %copy-start.4 = (s32[512,3]{0,1:T(4,128)S(1)}, s32[512,3]{0,1:T(4,128)}, u32[]{:S(2)}) copy-start(s32[512,3]{0,1:T(4,128)} %param.8) | copy-start | bytes 18436
  559.8 75.7 %copy-start.3 = (bf16[1,32768]{1,0:T(2,128)(2,1)S(1)}, bf16[1,32768]{1,0:T(2,128)(2,1)}, u32[]{:S(2)}) copy-start(bf16[1,32768]{1,0:T(2,128)(2,1)} %param.7) | copy-start | bytes 196612
  559.8 243.0 %all-to-all-start.1 = ((f32[32,1,32768]{2,1,0:T(1,128)}), f32[32,1,32768]{2,1,0:T(1,128)}, u32[]{:S(2)}, u32[]{:S(2)}) async-start(f32[32,1,32768]{2,1,0:T(1,128)} %reshape.149), calls=%async_computation.1 | async-start | bytes 8388608 | tf_op jit(solution)/shard_map/all_to_all | solution.py:64
  802.8 27.0 %all-to-all-start.2 = ((bf16[32,2,512]{2,1,0:T(2,128)(2,1)}), bf16[32,2,512]{2,1,0:T(2,128)(2,1)S(1)}, u32[]{:S(2)}, u32[]{:S(2)}) async-start(bf16[32,2,512]{2,1,0:T(2,128)(2,1)} %reshape.271), calls=%async_computation.2 | async-start | bytes 131072 | tf_op jit(solution)/shard_map/all_to_all | solution.py:208
  822.1 45.2 %copy-start.2 = (f32[32768]{0:T(1024)}, f32[32768]{0:T(1024)S(1)}, u32[]{:S(2)}) copy-start(f32[32768]{0:T(1024)S(1)} %reduce_sum.28) | copy-start | bytes 393220
  829.8 20.5 %all-to-all-start.3 = ((bf16[32,2,512]{2,1,0:T(2,128)(2,1)}), bf16[32,2,512]{2,1,0:T(2,128)(2,1)S(1)}, u32[]{:S(2)}, u32[]{:S(2)}) async-start(bf16[32,2,512]{2,1,0:T(2,128)(2,1)} %reshape.269), calls=%async_computation.3 | async-start | bytes 131072 | tf_op jit(solution)/shard_map/all_to_all | solution.py:154
Sparse Core Ops, SparseCore 0:
  27.5 263.5 all-gather.2
